TPU v7x, 32 devices: a whole 2x2x4 slice. The times are simulated.
32 devices in a mesh: sec: 8 (over y, x, core), strip: 4 (over z).
Axes of the slice: x: 2, y: 2, z: 4, core: 2. Of those that a mesh axis runs over, the one named last changes fastest.
Arguments:
- images: bfloat16 [8, 512, 1024], P('sec', 'strip'), may hold values from -6 to 6
- row_weights: float32 [8, 4, 512], P('sec', None, 'strip'), may hold values from 0.05 to 0.5
- row_shift: int32 [8, 4], P('sec', 'strip'), may hold values from -4 to 4
- col_weights: bfloat16 [8, 4, 1024], P('sec'), may hold values from 0.049804688 to 0.5
- col_shift: int32 [8], P('sec'), may hold values from -32 to 32
- pair_on: int32 [8, 3], replicated, may hold values 0 or 1
Outputs:
- grad_warped: float32 [8, 512, 1024], P('sec', 'strip')
- displacement: float32 [2, 8, 512, 1024], P(None, 'sec', 'strip')
All inputs are finite; a program needn't handle non-finite values.
Results may differ from a plain program's by a relative error of at most 0.0047.
Values may be sent and summed in bfloat16 or wider, within the bound.
A program may use at most 64 MiB of HBM per device.

v0:
```python
import jax
import jax.numpy as jnp
from jax import lax
from jax.sharding import PartitionSpec as P

TAP_COUNT = 4
MAX_SHIFT = 4
RADIUS = 4
PAIR_REACH = 3


variance_bias = 0.25


def padded_2(block, sides, width):
    for axis, dim in sides:
        count = lax.axis_size(axis)
        forward = [(i, i + 1) for i in range(count - 1)]
        backward = [(target, source) for source, target in forward]
        low = lax.ppermute(
            lax.slice_in_dim(block, block.shape[dim] - width, None, axis=dim), axis, forward
        )
        high = lax.ppermute(lax.slice_in_dim(block, 0, width, axis=dim), axis, backward)
        block = jnp.concatenate([low, block, high], axis=dim)
    return block


def passed_along(value, axis, steps):
    count = lax.axis_size(axis)
    initial, last = (max(0, -steps), min(count, count - steps))
    return lax.ppermute(value, axis, [(source, source + steps) for source in range(initial, last)])


def box_rows(field, out_rows):
    running = field[..., 0:out_rows, :]
    for step_row in range(1, 2 * RADIUS + 1):
        running = running + field[..., step_row : step_row + out_rows, :]
    return running


def box_cols(field):
    col_count = field.shape[-1]
    widths = [(0, 0)] * (field.ndim - 1) + [(RADIUS, RADIUS)]
    padded = jnp.pad(field, widths)
    running = padded[..., 0:col_count]
    for step_col in range(1, 2 * RADIUS + 1):
        running = running + padded[..., step_col : step_col + col_count]
    return running


def box_sum(field, out_rows):
    return box_cols(box_rows(field, out_rows))


def pair_grads(left_rim, right_rim, weight, depth, row_count):
    box_cells = float((2 * RADIUS + 1) ** 2)
    left_field = left_rim.astype(jnp.float32)
    right_field = right_rim.astype(jnp.float32)
    mean_left = box_sum(left_field, row_count) / box_cells
    mean_right = box_sum(right_field, row_count) / box_cells
    var_left = (
        box_sum(left_field * left_field, row_count) / box_cells
        - mean_left * mean_left
        + variance_bias
    )
    var_right = (
        box_sum(right_field * right_field, row_count) / box_cells
        - mean_right * mean_right
        + variance_bias
    )
    covariance = box_sum(left_field * right_field, row_count) / box_cells - mean_left * mean_right
    denom_root = jnp.sqrt(var_left * var_right)
    ncc_value = covariance / denom_root
    g_cov = -weight / denom_root
    g_left = weight * ncc_value / (2.0 * var_left)
    g_right = weight * ncc_value / (2.0 * var_right)
    h_left = -g_cov * mean_right - 2.0 * g_left * mean_left
    h_right = -g_cov * mean_left - 2.0 * g_right * mean_right
    stacked = jnp.stack([g_cov, g_left, g_right, h_left, h_right])
    widened = padded_2(stacked.astype(jnp.bfloat16), (("strip", 1),), RADIUS).astype(stacked.dtype)
    boxed = box_sum(widened, row_count)
    mid_left = left_field[depth : depth + row_count]
    mid_right = right_field[depth : depth + row_count]
    grad_left = (boxed[3] + 2.0 * mid_left * boxed[1] + mid_right * boxed[0]) / box_cells
    grad_right = (boxed[4] + 2.0 * mid_right * boxed[2] + mid_left * boxed[0]) / box_cells
    return (grad_left, grad_right)


def per_device(images, row_weights, row_shift, col_weights, col_shift, pair_on):
    sec_count, row_count, col_count = images.shape
    sec_pos = lax.axis_index("sec")
    total_sections = sec_count * lax.axis_size("sec")
    source_depth = MAX_SHIFT + 2
    source = padded_2(images, (("strip", 1),), source_depth)

    def warp_rows(source_sec, weights, shift_value):
        running = jnp.zeros((row_count, col_count), jnp.float32)
        for tap_index in range(TAP_COUNT):
            window = lax.dynamic_slice_in_dim(
                source_sec, source_depth - 1 + tap_index + shift_value, row_count, 0
            )
            running = running + weights[tap_index][:, None] * window.astype(jnp.float32)
        return running.astype(jnp.bfloat16)

    row_warped = jax.vmap(warp_rows)(source, row_weights, row_shift[:, 0])
    row_ids = lax.broadcasted_iota(jnp.int32, (col_count, col_count), 0)
    col_ids = lax.broadcasted_iota(jnp.int32, (col_count, col_count), 1)

    def column_matrix(weights, shift_value):
        offsets = row_ids - col_ids - shift_value + 1
        matrix = jnp.zeros((col_count, col_count), jnp.bfloat16)
        for tap_index in range(TAP_COUNT):
            matrix = jnp.where(offsets == tap_index, weights[tap_index][None, :], matrix)
        return matrix

    matrices = jax.vmap(column_matrix)(col_weights, col_shift)
    warped = jnp.einsum(
        "srw,swv->srv", row_warped, matrices, preferred_element_type=jnp.float32
    ).astype(jnp.bfloat16)
    depth = RADIUS
    rimmed = padded_2(warped, (("strip", 1),), depth)
    hops = (PAIR_REACH + sec_count - 1) // sec_count
    first_global = sec_pos * sec_count
    padded_on = jnp.concatenate([jnp.zeros((PAIR_REACH, PAIR_REACH), jnp.int32), pair_on], 0)
    on_rows = lax.dynamic_slice_in_dim(padded_on, first_global, sec_count + PAIR_REACH, 0).astype(
        jnp.float32
    )
    pieces = {}
    section = 0
    pieces[section] = rimmed[section]
    for hop in range(1, hops + 1):
        arrived = passed_along(rimmed, "sec", -hop)
        slot_pos = 0
        pieces[hop * sec_count + slot_pos] = arrived[slot_pos]
    gradient_sums = {}
    section = 0
    for distance in range(1, PAIR_REACH + 1):
        global_first = first_global + section
        inside = (global_first >= 0) & (global_first + distance < total_sections)
        grad_left, grad_right = pair_grads(
            pieces[section],
            pieces[section + distance],
            on_rows[section + PAIR_REACH, distance - 1] * inside.astype(jnp.float32),
            depth,
            row_count,
        )
        for target, term in ((section, grad_left), (section + distance, grad_right)):
            if target in gradient_sums:
                gradient_sums[target] = gradient_sums[target] + term
            else:
                gradient_sums[target] = term
    section = 0
    own_grads = [gradient_sums[section]]
    for hop in range(1, hops + 1):
        parcel = jnp.stack([gradient_sums[hop * sec_count]])
        returned = passed_along(parcel, "sec", hop)
        slot_pos = 0
        own_grads[slot_pos] = own_grads[slot_pos] + returned[slot_pos]
    grad_warped = jnp.stack(own_grads)
    middle = rimmed[:, depth - 1 : depth + row_count + 1].astype(jnp.float32)
    slope_rows = (middle[:, 2:] - middle[:, :-2]) * 0.5
    centre = middle[:, 1:-1]
    side_padded = jnp.pad(centre, ((0, 0), (0, 0), (1, 1)))
    slope_cols = (side_padded[:, :, 2:] - side_padded[:, :, :-2]) * 0.5
    products = jnp.stack([grad_warped * slope_rows, grad_warped * slope_cols])
    widened = padded_2(products, (("strip", 2),), RADIUS)
    displacement = -box_sum(widened, row_count) / 9.0
    return (grad_warped, displacement)


def solution(mesh):
    return jax.shard_map(
        per_device,
        mesh=mesh,
        in_specs=(
            P("sec", "strip", None),
            P("sec", None, "strip"),
            P("sec", "strip"),
            P("sec", None, None),
            P("sec"),
            P(),
        ),
        out_specs=(P("sec", "strip", None), P(None, "sec", "strip", None)),
        check_vma=False,
    )
```

profile of v0, /device:TPU:4, one launch (start us, length us, event | category | flops | bytes accessed | tf_op | source)
XLA Modules:
  0.0 148.2 jit_solution(8800515627362992691)
XLA Ops:
  1.4 3.5 %collective-permute-start = (bf16[1,6,1024]{2,1,0:T(8,128)(2,1)S(1)}, bf16[1,6,1024]{2,1,0:T(8,128)(2,1)S(1)}, u32[]{:S(2)}, u32[]{:S(2)}) collective-permute-start(bf16[1,6,1024]{2,1,0:T(8,128)(2,1)S(1)} %get-tuple-element.109), channel_id=1, source_target_pairs={{0,1},{1,2},{2,3},{4,5},{5,6},{6,7},{8,9},{9,10},{10,11},{12,13},{... | collective-permute-start | bytes 36872 | tf_op jit(solution)/shard_map/ppermute | solution.py:20
  11.5 2.3 %fusion.37 = bf16[1,128,1024]{2,1,0:T(8,128)(2,1)S(1)} fusion(s32[]{:T(128)} %bitcast.118, bf16[1024]{0:T(1024)(128)(2,1)S(1)} %get-tuple-element.48, bf16[1024]{0:T(1024)(128)(2,1)S(1)} %get-tuple-element.49, bf16[1024]{0:T(1024)(128)(2,1)S(1)} %get-tuple-element.47, bf16[1024]{0:T(1024)(128)(2,1)S(1)} %get-tuple-element.46, ...), kind=kOutput, calls=%fused_computation.91 | convolution fusion | flops 281673728 | bytes 1320980 | tf_op jit(solution)/shard_map/srw,swv->srv/dot_general | solution.py:117
  13.9 3.5 %collective-permute-start.2 = (bf16[1,4,1024]{2,1,0:T(4,128)(2,1)S(1)}, bf16[1,4,1024]{2,1,0:T(4,128)(2,1)S(1)}, u32[]{:S(2)}, u32[]{:S(2)}) collective-permute-start(bf16[1,4,1024]{2,1,0:T(4,128)(2,1)S(1)} %get-tuple-element.107), channel_id=1, source_target_pairs={{0,1},{1,2},{2,3},{4,5},{5,6},{6,7},{8,9},{9,10},{10,11},{12,13},{... | collective-permute-start | bytes 24584 | tf_op jit(solution)/shard_map/ppermute | solution.py:20
  18.8 4.1 %collective-permute-done.3 = bf16[1,4,1024]{2,1,0:T(4,128)(2,1)S(1)} collective-permute-done((bf16[1,4,1024]{2,1,0:T(4,128)(2,1)S(1)}, bf16[1,4,1024]{2,1,0:T(4,128)(2,1)S(1)}, u32[]{:S(2)}, u32[]{:S(2)}) %collective-permute-start.3) | collective-permute-done | bytes 8224 | tf_op jit(solution)/shard_map/ppermute | solution.py:23
  23.0 3.3 %collective-permute-start.7 = (bf16[1,136,1024]{2,1,0:T(8,128)(2,1)S(1)}, bf16[1,136,1024]{2,1,0:T(8,128)(2,1)S(1)}, u32[]{:S(2)}, u32[]{:S(2)}) collective-permute-start(bf16[1,136,1024]{2,1,0:T(8,128)(2,1)S(1)} %get-tuple-element.106), channel_id=1, source_target_pairs={{8,0},{12,4},{16,8},{20,12},{24,16},{28,20},{9,1},{13,5},{17,9},{2... | collective-permute-start | bytes 835592 | tf_op jit(solution)/shard_map/ppermute | solution.py:31
  33.5 3.3 %collective-permute-done.10 = bf16[1,136,1024]{2,1,0:T(8,128)(2,1)S(1)} collective-permute-done((bf16[1,136,1024]{2,1,0:T(8,128)(2,1)S(1)}, bf16[1,136,1024]{2,1,0:T(8,128)(2,1)S(1)}, u32[]{:S(2)}, u32[]{:S(2)}) %collective-permute-start.10) | collective-permute-done | bytes 278560 | tf_op jit(solution)/shard_map/ppermute | solution.py:31
  41.4 4.8 %bitcast_dynamic-update-slice_fusion.8 = (bf16[5,128,1024]{2,1,0:T(8,128)(2,1)S(1)}, f32[128,1024]{1,0:T(8,128)S(1)}, f32[128,1024]{1,0:T(8,128)S(1)}, f32[128,1...) fusion(f32[]{:T(128)S(6)} %neg.24, f32[128,1024]{1,0:T(8,128)S(1)} %get-tuple-element.123, ...), kind=kLoop, calls=%fused_computation.522 | loop fusion | flops 5898239 | bytes 4980740
  46.1 2.2 %bitcast_dynamic-update-slice_fusion.5 = (bf16[5,128,1024]{2,1,0:T(8,128)(2,1)S(1)}, f32[128,1024]{1,0:T(8,128)S(1)}, f32[128,1024]{1,0:T(8,128)S(1)}, f32[128,1024]{1,0:T(8,128)S(1)}) fusion(f32[128,1024]{1,0:T(8,128)S(1)} %get-tuple-element.58, f32[]{:T(128)S(6)} %neg.26, f32[128,1024]{1,0:T(8,128)S(1)} %get-tuple-element.121, f32[128,1024]{1,0:T(8,128)S(1)} %fusion.204), kind=kLoop, calls=%fused_computation.519 | loop fusion | flops 3145727 | bytes 3407876
  48.4 4.6 %bitcast_dynamic-update-slice_fusion.7 = (bf16[5,128,1024]{2,1,0:T(8,128)(2,1)S(1)}, f32[128,1024]{1,0:T(8,128)S(1)}, bf16[5,128,1024]{2,1,0:T(8,128)(2,1)S(1)},...) fusion(bf16[5,128,1024]{2,1,0:T(8,128)(2,1)S(1)} %get-tuple-ele, ...), kind=kLoop, calls=%fused_computation.521 | loop fusion | flops 7471103 | bytes 8650764
  56.0 3.5 %collective-permute-start.11 = (bf16[5,4,1024]{2,1,0:T(4,128)(2,1)S(1)}, bf16[5,4,1024]{2,1,0:T(4,128)(2,1)S(1)}, u32[]{:S(2)}, u32[]{:S(2)}) collective-permute-start(bf16[5,4,1024]{2,1,0:T(4,128)(2,1)S(1)} %get-tuple-element.76), channel_id=1, source_target_pairs={{0,1},{1,2},{2,3},{4,5},{5,6},{6,7},{8,9},{9,10},{10,11},{12,13},{... | collective-permute-start | bytes 122888 | tf_op jit(solution)/shard_map/ppermute | solution.py:20
  60.9 4.5 %collective-permute-start.8 = (bf16[5,4,1024]{2,1,0:T(4,128)(2,1)S(1)}, bf16[5,4,1024]{2,1,0:T(4,128)(2,1)S(1)}, u32[]{:S(2)}, u32[]{:S(2)}) collective-permute-start(bf16[5,4,1024]{2,1,0:T(4,128)(2,1)S(1)} %get-tuple-element.74), channel_id=1, source_target_pairs={{0,1},{1,2},{2,3},{4,5},{5,6},{6,7},{8,9},{9,10},{10,11},{12,13},{... | collective-permute-start | bytes 122888 | tf_op jit(solution)/shard_map/ppermute | solution.py:20
  66.8 4.5 %collective-permute-start.5 = (bf16[5,4,1024]{2,1,0:T(4,128)(2,1)S(1)}, bf16[5,4,1024]{2,1,0:T(4,128)(2,1)S(1)}, u32[]{:S(2)}, u32[]{:S(2)}) collective-permute-start(bf16[5,4,1024]{2,1,0:T(4,128)(2,1)S(1)} %get-tuple-element.72), channel_id=1, source_target_pairs={{0,1},{1,2},{2,3},{4,5},{5,6},{6,7},{8,9},{9,10},{10,11},{12,13},{... | collective-permute-start | bytes 122888 | tf_op jit(solution)/shard_map/ppermute | solution.py:20
  73.1 2.1 %slice_add_fusion = f32[5,128,1024]{2,1,0:T(8,128)S(1)} fusion(f32[5,136,1024]{2,1,0:T(8,128)S(1)} %maximum_convert_fusion.2), kind=kLoop, calls=%fused_computation.57 | loop fusion | flops 5242880 | bytes 26214400 | tf_op jit(solution)/shard_map/add | solution.py:37
  75.2 5.6 %fusion.31 = f32[5,128,1024]{2,1,0:T(8,128)S(1)} fusion(f32[5,128,1024]{2,1,0:T(8,128)S(1)} %slice_add_fusion), kind=kLoop, calls=%fused_computation.56 | loop fusion | flops 5242880 | bytes 5242880 | tf_op jit(solution)/shard_map/add | solution.py:47
  83.2 5.6 %fusion.23 = f32[5,128,1024]{2,1,0:T(8,128)S(1)} fusion(f32[5,128,1024]{2,1,0:T(8,128)S(1)} %slice_add_fusion.8), kind=kLoop, calls=%fused_computation.48 | loop fusion | flops 5242880 | bytes 5242880 | tf_op jit(solution)/shard_map/add | solution.py:47
  91.1 5.8 %fusion.15 = f32[5,128,1024]{2,1,0:T(8,128)S(1)} fusion(f32[5,128,1024]{2,1,0:T(8,128)S(1)} %slice_add_fusion.16), kind=kLoop, calls=%fused_computation.40 | loop fusion | flops 5242880 | bytes 5242880 | tf_op jit(solution)/shard_map/add | solution.py:47
  97.8 2.2 %collective-permute-start.13 = (f32[1,128,1024]{2,1,0:T(8,128)S(1)}, f32[1,128,1024]{2,1,0:T(8,128)S(1)}, u32[]{:S(2)}, u32[]{:S(2)}) collective-permute-start(f32[1,128,1024]{2,1,0:T(8,128)S(1)} %get-tuple-element.88), channel_id=1, source_target_pairs={{0,4},{4,8},{8,12},{12,16},{16,20},{20,24},{24,28},{1,5},{5,9},{9,... | collective-permute-start | bytes 1572872 | tf_op jit(solution)/shard_map/ppermute | solution.py:31
  100.0 5.1 %collective-permute-start.14 = (f32[1,128,1024]{2,1,0:T(8,128)S(1)}, f32[1,128,1024]{2,1,0:T(8,128)S(1)}, u32[]{:S(2)}, u32[]{:S(2)}) collective-permute-start(f32[1,128,1024]{2,1,0:T(8,128)S(1)} %get-tuple-element.89), channel_id=1, source_target_pairs={{0,8},{4,12},{8,16},{12,20},{16,24},{20,28},{1,9},{5,13},{9,17},{1... | collective-permute-start | bytes 1572872 | tf_op jit(solution)/shard_map/ppermute | solution.py:31
  107.1 5.9 %collective-permute-done.13 = f32[1,128,1024]{2,1,0:T(8,128)S(1)} collective-permute-done((f32[1,128,1024]{2,1,0:T(8,128)S(1)}, f32[1,128,1024]{2,1,0:T(8,128)S(1)}, u32[]{:S(2)}, u32[]{:S(2)}) %collective-permute-start.13) | collective-permute-done | bytes 524320 | tf_op jit(solution)/shard_map/ppermute | solution.py:31
  113.0 5.3 %collective-permute-done.14 = f32[1,128,1024]{2,1,0:T(8,128)S(1)} collective-permute-done((f32[1,128,1024]{2,1,0:T(8,128)S(1)}, f32[1,128,1024]{2,1,0:T(8,128)S(1)}, u32[]{:S(2)}, u32[]{:S(2)}) %collective-permute-start.14) | collective-permute-done | bytes 524320 | tf_op jit(solution)/shard_map/ppermute | solution.py:31
  118.4 14.1 %collective-permute-done.15 = f32[1,128,1024]{2,1,0:T(8,128)S(1)} collective-permute-done((f32[1,128,1024]{2,1,0:T(8,128)S(1)}, f32[1,128,1024]{2,1,0:T(8,128)S(1)}, u32[]{:S(2)}, u32[]{:S(2)}) %collective-permute-start.15) | collective-permute-done | bytes 524320 | tf_op jit(solution)/shard_map/ppermute | solution.py:31
  133.9 4.3 %collective-permute-start.16 = (f32[2,1,4,1024]{3,2,1,0:T(4,128)S(1)}, f32[2,1,4,1024]{3,2,1,0:T(4,128)S(1)}, u32[]{:S(2)}, u32[]{:S(2)}) collective-permute-start(f32[2,1,4,1024]{3,2,1,0:T(4,128)S(1)} %get-tuple-element.80), channel_id=1, source_target_pairs={{0,1},{1,2},{2,3},{4,5},{5,6},{6,7},{8,9},{9,10},{10,11},{12,13},{... | collective-permute-start | bytes 98312 | tf_op jit(solution)/shard_map/ppermute | solution.py:20
  139.8 4.2 %collective-permute-done.17 = f32[2,1,4,1024]{3,2,1,0:T(4,128)S(1)} collective-permute-done((f32[2,1,4,1024]{3,2,1,0:T(4,128)S(1)}, f32[2,1,4,1024]{3,2,1,0:T(4,128)S(1)}, u32[]{:S(2)}, u32[]{:S(2)}) %collective-permute-start.17) | collective-permute-done | bytes 32800 | tf_op jit(solution)/shard_map/ppermute | solution.py:23
  145.0 3.2 %fusion.49 = f32[2,1,128,1024]{3,2,1,0:T(8,128)} fusion(f32[2,1,128,1024]{3,2,1,0:T(8,128)S(1)} %fusion.54), kind=kLoop, calls=%fused_computation.111 | loop fusion | flops 2621440 | bytes 2097152 | tf_op jit(solution)/shard_map/div | solution.py:167
  (65 shorter events, 36.2 us)
Async XLA Ops:
  1.4 7.8 %collective-permute-start = (bf16[1,6,1024]{2,1,0:T(8,128)(2,1)S(1)}, bf16[1,6,1024]{2,1,0:T(8,128)(2,1)S(1)}, u32[]{:S(2)}, u32[]{:S(2)}) collective-permute-start(bf16[1,6,1024]{2,1,0:T(8,128)(2,1)S(1)} %get-tuple-element.109), channel_id=1, source_target_pairs={{0,1},{1,2},{2,3},{4,5},{5,6},{6,7},{8,9},{9,10},{10,11},{12,13},{... | collective-permute-start | bytes 36872 | tf_op jit(solution)/shard_map/ppermute | solution.py:20
  4.9 5.6 %collective-permute-start.1 = (bf16[1,6,1024]{2,1,0:T(8,128)(2,1)S(1)}, bf16[1,6,1024]{2,1,0:T(8,128)(2,1)S(1)}, u32[]{:S(2)}, u32[]{:S(2)}) collective-permute-start(bf16[1,6,1024]{2,1,0:T(8,128)(2,1)S(1)} %get-tuple-element.110), channel_id=1, source_target_pairs={{1,0},{2,1},{3,2},{5,4},{6,5},{7,6},{9,8},{10,9},{11,10},{13,12},{... | collective-permute-start | bytes 36872 | tf_op jit(solution)/shard_map/ppermute | solution.py:23
  11.5 7.2 %copy-start.1 = (s32[8,3]{0,1:T(4,128)S(1)}, s32[8,3]{0,1:T(4,128)}, u32[]{:S(2)}) copy-start(s32[8,3]{0,1:T(4,128)} %param.11) | copy-start | bytes 292
  13.9 4.9 %collective-permute-start.2 = (bf16[1,4,1024]{2,1,0:T(4,128)(2,1)S(1)}, bf16[1,4,1024]{2,1,0:T(4,128)(2,1)S(1)}, u32[]{:S(2)}, u32[]{:S(2)}) collective-permute-start(bf16[1,4,1024]{2,1,0:T(4,128)(2,1)S(1)} %get-tuple-element.107), channel_id=1, source_target_pairs={{0,1},{1,2},{2,3},{4,5},{5,6},{6,7},{8,9},{9,10},{10,11},{12,13},{... | collective-permute-start | bytes 24584 | tf_op jit(solution)/shard_map/ppermute | solution.py:20
  17.4 5.5 %collective-permute-start.3 = (bf16[1,4,1024]{2,1,0:T(4,128)(2,1)S(1)}, bf16[1,4,1024]{2,1,0:T(4,128)(2,1)S(1)}, u32[]{:S(2)}, u32[]{:S(2)}) collective-permute-start(bf16[1,4,1024]{2,1,0:T(4,128)(2,1)S(1)} %get-tuple-element.108), channel_id=1, source_target_pairs={{1,0},{2,1},{3,2},{5,4},{6,5},{7,6},{9,8},{10,9},{11,10},{13,12},{... | collective-permute-start | bytes 24584 | tf_op jit(solution)/shard_map/ppermute | solution.py:23
  23.0 10.1 %collective-permute-start.7 = (bf16[1,136,1024]{2,1,0:T(8,128)(2,1)S(1)}, bf16[1,136,1024]{2,1,0:T(8,128)(2,1)S(1)}, u32[]{:S(2)}, u32[]{:S(2)}) collective-permute-start(bf16[1,136,1024]{2,1,0:T(8,128)(2,1)S(1)} %get-tuple-element.106), channel_id=1, source_target_pairs={{8,0},{12,4},{16,8},{20,12},{24,16},{28,20},{9,1},{13,5},{17,9},{2... | collective-permute-start | bytes 835592 | tf_op jit(solution)/shard_map/ppermute | solution.py:31
  28.9 8.0 %collective-permute-start.10 = (bf16[1,136,1024]{2,1,0:T(8,128)(2,1)S(1)}, bf16[1,136,1024]{2,1,0:T(8,128)(2,1)S(1)}, u32[]{:S(2)}, u32[]{:S(2)}) collective-permute-start(bf16[1,136,1024]{2,1,0:T(8,128)(2,1)S(1)} %get-tuple-element.106), channel_id=1, source_target_pairs={{12,0},{16,4},{20,8},{24,12},{28,16},{13,1},{17,5},{21,9},{25,13},... | collective-permute-start | bytes 835592 | tf_op jit(solution)/shard_map/ppermute | solution.py:31
  30.8 7.0 %collective-permute-start.4 = (bf16[1,136,1024]{2,1,0:T(8,128)(2,1)S(1)}, bf16[1,136,1024]{2,1,0:T(8,128)(2,1)S(1)}, u32[]{:S(2)}, u32[]{:S(2)}) collective-permute-start(bf16[1,136,1024]{2,1,0:T(8,128)(2,1)S(1)} %get-tuple-element.106), channel_id=1, source_target_pairs={{4,0},{8,4},{12,8},{16,12},{20,16},{24,20},{28,24},{5,1},{9,5},{13... | collective-permute-start | bytes 835592 | tf_op jit(solution)/shard_map/ppermute | solution.py:31
  56.0 15.3 %collective-permute-start.11 = (bf16[5,4,1024]{2,1,0:T(4,128)(2,1)S(1)}, bf16[5,4,1024]{2,1,0:T(4,128)(2,1)S(1)}, u32[]{:S(2)}, u32[]{:S(2)}) collective-permute-start(bf16[5,4,1024]{2,1,0:T(4,128)(2,1)S(1)} %get-tuple-element.76), channel_id=1, source_target_pairs={{0,1},{1,2},{2,3},{4,5},{5,6},{6,7},{8,9},{9,10},{10,11},{12,13},{... | collective-permute-start | bytes 122888 | tf_op jit(solution)/shard_map/ppermute | solution.py:20
  59.5 13.1 %collective-permute-start.12 = (bf16[5,4,1024]{2,1,0:T(4,128)(2,1)S(1)}, bf16[5,4,1024]{2,1,0:T(4,128)(2,1)S(1)}, u32[]{:S(2)}, u32[]{:S(2)}) collective-permute-start(bf16[5,4,1024]{2,1,0:T(4,128)(2,1)S(1)} %get-tuple-element.77), channel_id=1, source_target_pairs={{1,0},{2,1},{3,2},{5,4},{6,5},{7,6},{9,8},{10,9},{11,10},{13,12},{... | collective-permute-start | bytes 122888 | tf_op jit(solution)/shard_map/ppermute | solution.py:23
  60.9 19.9 %collective-permute-start.8 = (bf16[5,4,1024]{2,1,0:T(4,128)(2,1)S(1)}, bf16[5,4,1024]{2,1,0:T(4,128)(2,1)S(1)}, u32[]{:S(2)}, u32[]{:S(2)}) collective-permute-start(bf16[5,4,1024]{2,1,0:T(4,128)(2,1)S(1)} %get-tuple-element.74), channel_id=1, source_target_pairs={{0,1},{1,2},{2,3},{4,5},{5,6},{6,7},{8,9},{9,10},{10,11},{12,13},{... | collective-permute-start | bytes 122888 | tf_op jit(solution)/shard_map/ppermute | solution.py:20
  65.4 15.4 %collective-permute-start.9 = (bf16[5,4,1024]{2,1,0:T(4,128)(2,1)S(1)}, bf16[5,4,1024]{2,1,0:T(4,128)(2,1)S(1)}, u32[]{:S(2)}, u32[]{:S(2)}) collective-permute-start(bf16[5,4,1024]{2,1,0:T(4,128)(2,1)S(1)} %get-tuple-element.75), channel_id=1, source_target_pairs={{1,0},{2,1},{3,2},{5,4},{6,5},{7,6},{9,8},{10,9},{11,10},{13,12},{... | collective-permute-start | bytes 122888 | tf_op jit(solution)/shard_map/ppermute | solution.py:23
  66.8 22.0 %collective-permute-start.5 = (bf16[5,4,1024]{2,1,0:T(4,128)(2,1)S(1)}, bf16[5,4,1024]{2,1,0:T(4,128)(2,1)S(1)}, u32[]{:S(2)}, u32[]{:S(2)}) collective-permute-start(bf16[5,4,1024]{2,1,0:T(4,128)(2,1)S(1)} %get-tuple-element.72), channel_id=1, source_target_pairs={{0,1},{1,2},{2,3},{4,5},{5,6},{6,7},{8,9},{9,10},{10,11},{12,13},{... | collective-permute-start | bytes 122888 | tf_op jit(solution)/shard_map/ppermute | solution.py:20
  71.3 17.4 %collective-permute-start.6 = (bf16[5,4,1024]{2,1,0:T(4,128)(2,1)S(1)}, bf16[5,4,1024]{2,1,0:T(4,128)(2,1)S(1)}, u32[]{:S(2)}, u32[]{:S(2)}) collective-permute-start(bf16[5,4,1024]{2,1,0:T(4,128)(2,1)S(1)} %get-tuple-element.73), channel_id=1, source_target_pairs={{1,0},{2,1},{3,2},{5,4},{6,5},{7,6},{9,8},{10,9},{11,10},{13,12},{... | collective-permute-start | bytes 122888 | tf_op jit(solution)/shard_map/ppermute | solution.py:23
  97.8 15.2 %collective-permute-start.13 = (f32[1,128,1024]{2,1,0:T(8,128)S(1)}, f32[1,128,1024]{2,1,0:T(8,128)S(1)}, u32[]{:S(2)}, u32[]{:S(2)}) collective-permute-start(f32[1,128,1024]{2,1,0:T(8,128)S(1)} %get-tuple-element.88), channel_id=1, source_target_pairs={{0,4},{4,8},{8,12},{12,16},{16,20},{20,24},{24,28},{1,5},{5,9},{9,... | collective-permute-start | bytes 1572872 | tf_op jit(solution)/shard_map/ppermute | solution.py:31
  100.0 18.4 %collective-permute-start.14 = (f32[1,128,1024]{2,1,0:T(8,128)S(1)}, f32[1,128,1024]{2,1,0:T(8,128)S(1)}, u32[]{:S(2)}, u32[]{:S(2)}) collective-permute-start(f32[1,128,1024]{2,1,0:T(8,128)S(1)} %get-tuple-element.89), channel_id=1, source_target_pairs={{0,8},{4,12},{8,16},{12,20},{16,24},{20,28},{1,9},{5,13},{9,17},{1... | collective-permute-start | bytes 1572872 | tf_op jit(solution)/shard_map/ppermute | solution.py:31
  105.1 27.3 %collective-permute-start.15 = (f32[1,128,1024]{2,1,0:T(8,128)S(1)}, f32[1,128,1024]{2,1,0:T(8,128)S(1)}, u32[]{:S(2)}, u32[]{:S(2)}) collective-permute-start(f32[1,128,1024]{2,1,0:T(8,128)S(1)} %get-tuple-element.90), channel_id=1, source_target_pairs={{0,12},{4,16},{8,20},{12,24},{16,28},{1,13},{5,17},{9,21},{13,25},... | collective-permute-start | bytes 1572872 | tf_op jit(solution)/shard_map/ppermute | solution.py:31
  133.6 10.7 %copy-start = (f32[1,128,1024]{2,1,0:T(8,128)}, f32[1,128,1024]{2,1,0:T(8,128)S(1)}, u32[]{:S(2)}) copy-start(f32[1,128,1024]{2,1,0:T(8,128)S(1)} %get-tuple-element.51) | copy-start | bytes 1572868
  133.9 5.9 %collective-permute-start.16 = (f32[2,1,4,1024]{3,2,1,0:T(4,128)S(1)}, f32[2,1,4,1024]{3,2,1,0:T(4,128)S(1)}, u32[]{:S(2)}, u32[]{:S(2)}) collective-permute-start(f32[2,1,4,1024]{3,2,1,0:T(4,128)S(1)} %get-tuple-element.80), channel_id=1, source_target_pairs={{0,1},{1,2},{2,3},{4,5},{5,6},{6,7},{8,9},{9,10},{10,11},{12,13},{... | collective-permute-start | bytes 98312 | tf_op jit(solution)/shard_map/ppermute | solution.py:20
  138.2 5.8 %collective-permute-start.17 = (f32[2,1,4,1024]{3,2,1,0:T(4,128)S(1)}, f32[2,1,4,1024]{3,2,1,0:T(4,128)S(1)}, u32[]{:S(2)}, u32[]{:S(2)}) collective-permute-start(f32[2,1,4,1024]{3,2,1,0:T(4,128)S(1)} %get-tuple-element.81), channel_id=1, source_target_pairs={{1,0},{2,1},{3,2},{5,4},{6,5},{7,6},{9,8},{10,9},{11,10},{13,12},{... | collective-permute-start | bytes 98312 | tf_op jit(solution)/shard_map/ppermute | solution.py:23
where the time goes:
time: 149 us; the launch traced here: 148 us
  other arithmetic  51.2 us (34%)
  starting transfers between devices  48 us (32%)
  waiting for transfers between devices  39.1 us (26%)
  between operations  4.37 us (3%)
  local copies, waits for them, and re-layouts  3.21 us (2%)
  matrix products  2.34 us (2%)
    ppermute x6, waiting for transfers between devices, passed_along(): lax.ppermute(value, axis, [(source, source + steps) for source in range(i...  29.2 us
    ppermute x6, starting transfers between devices, padded_2(): lax.ppermute(lax.slice_in_dim(block, block.shape[dim] - width, None, axis...  23.8 us
    add x3, other arithmetic, box_cols(): running = running + padded[..., step_col:step_col + col_count]  16.9 us
    ppermute x6, starting transfers between devices, passed_along(): lax.ppermute(value, axis, [(source, source + steps) for source in range(i...  16.4 us
    unnamed x8, other arithmetic  13.7 us
    add x11, other arithmetic, box_rows(): running = running + field[..., step_row:step_row + out_rows, :]  10.8 us
    ppermute x6, waiting for transfers between devices, padded_2(): lax.ppermute(lax.slice_in_dim(block, 0, width, axis=dim), axis, backward)  9.65 us
    ppermute x6, starting transfers between devices, padded_2(): lax.ppermute(lax.slice_in_dim(block, 0, width, axis=dim), axis, backward)  7.75 us
  transfers between devices with their start and end apart: 18, of which 9 were waited for; matrix products, arithmetic and copies ran while one was open for 13% of the time, Pallas kernels for 0%

commit v1 on v0

--- a/solution.py
+++ b/solution.py
@@ -1,6 +1,10 @@
+import functools
+
 import jax
 import jax.numpy as jnp
 from jax import lax
+from jax.experimental import pallas as pl
+from jax.experimental.pallas import tpu as pltpu
 from jax.sharding import PartitionSpec as P
 
 TAP_COUNT = 4
@@ -168,9 +172,390 @@
     return (grad_warped, displacement)
 
 
+MESH = pl.DeviceIdType.MESH
+BLOCK = 16
+LANES = 128
+COL_TILE = 256
+
+
+def rows_sum_from(x):
+    m = x.shape[0]
+    t = x + pltpu.roll(x, m - 1, 0) + pltpu.roll(x, m - 2, 0)
+    t = t + pltpu.roll(t, m - 3, 0) + pltpu.roll(t, m - 6, 0)
+    return t[: m - 2 * RADIUS]
+
+
+def rows_sum_centred(x):
+    m = x.shape[0]
+    t = x + pltpu.roll(x, m - 1, 0) + pltpu.roll(x, 1, 0)
+    return t + pltpu.roll(t, m - 3, 0) + pltpu.roll(t, 3, 0)
+
+
+def with_zero_lanes(x):
+    return jnp.concatenate([x, jnp.zeros((x.shape[0], LANES), x.dtype)], axis=1)
+
+
+def cols_sum(x):
+    width = x.shape[1]
+    x = with_zero_lanes(x)
+    m = width + LANES
+    t = x + pltpu.roll(x, m - 1, 1) + pltpu.roll(x, 1, 1)
+    t = t + pltpu.roll(t, m - 3, 1) + pltpu.roll(t, 3, 1)
+    return t[:, :width]
+
+
+def align_kernel(
+    n,
+    strips,
+    images,
+    row_weights,
+    row_shift,
+    col_weights,
+    col_shift,
+    pair_on,
+    grad_out,
+    disp_out,
+    img_ext,
+    col_mats,
+    warp_ext,
+    window,
+    field,
+    mean,
+    inv,
+    ncc_sum,
+    mean_sum,
+    grad_acc,
+    grad_send,
+    grad_ext,
+    img_send,
+    img_recv,
+    halo_send,
+    halo_recv,
+    win_send,
+    win_recv,
+    back_send,
+    back_recv,
+    edge_send,
+    edge_recv,
+):
+    me = lax.axis_index("sec")
+    z = lax.axis_index("strip")
+    rows, width = images.shape
+    f32, bf16 = jnp.float32, jnp.bfloat16
+    has_up = z > 0
+    has_down = z < strips - 1
+    up = {"strip": z - 1}
+    down = {"strip": z + 1}
+    cells = float((2 * RADIUS + 1) ** 2)
+
+    def remote(src, dst, send, recv, where):
+        return pltpu.make_async_remote_copy(
+            src_ref=src, dst_ref=dst, send_sem=send, recv_sem=recv, device_id=where, device_id_type=MESH
+        )
+
+    barrier = pltpu.get_barrier_semaphore()
+    for step in range(1, n):
+        pl.semaphore_signal(
+            barrier, inc=1, device_id={"sec": lax.rem(me + step, n)}, device_id_type=MESH
+        )
+
+    @pl.when(has_up)
+    def _():
+        pl.semaphore_signal(barrier, inc=1, device_id=up, device_id_type=MESH)
+
+    @pl.when(has_down)
+    def _():
+        pl.semaphore_signal(barrier, inc=1, device_id=down, device_id_type=MESH)
+
+    pl.semaphore_wait(barrier, n - 1 + jnp.where(has_up, 1, 0) + jnp.where(has_down, 1, 0))
+
+    img_up = remote(
+        images.at[pl.ds(0, BLOCK)], img_ext.at[pl.ds(rows + BLOCK, BLOCK)], img_send.at[0], img_recv.at[1], up
+    )
+    img_down = remote(
+        images.at[pl.ds(rows - BLOCK, BLOCK)], img_ext.at[pl.ds(0, BLOCK)], img_send.at[1], img_recv.at[0], down
+    )
+
+    def exchange_start(to_up, to_down):
+        @pl.when(has_up)
+        def _():
+            to_up.start()
+
+        @pl.when(has_down)
+        def _():
+            to_down.start()
+
+    def exchange_wait(to_up, to_down):
+        @pl.when(has_up)
+        def _():
+            to_up.wait_send()
+            to_down.wait_recv()
+
+        @pl.when(has_down)
+        def _():
+            to_down.wait_send()
+            to_up.wait_recv()
+
+    exchange_start(img_up, img_down)
+    zero_block = jnp.zeros((BLOCK, width), bf16)
+
+    @pl.when(jnp.logical_not(has_up))
+    def _():
+        img_ext[0:BLOCK] = zero_block
+        warp_ext[0] = zero_block
+        grad_ext[0] = zero_block
+
+    @pl.when(jnp.logical_not(has_down))
+    def _():
+        img_ext[rows + BLOCK : rows + 2 * BLOCK] = zero_block
+        warp_ext[n + 1] = zero_block
+        grad_ext[n + 1] = zero_block
+
+    img_ext[BLOCK : rows + BLOCK] = images[...]
+    col_move = col_shift[0]
+    spans = []
+    for tile in range(width // COL_TILE):
+        first = max(0, tile * COL_TILE - LANES)
+        last = min(width, (tile + 1) * COL_TILE + LANES)
+        spans.append((first, last))
+        extent = last - first
+        row_ids = lax.broadcasted_iota(jnp.int32, (extent, COL_TILE), 0) + first
+        col_ids = lax.broadcasted_iota(jnp.int32, (extent, COL_TILE), 1) + tile * COL_TILE
+        offsets = row_ids - col_ids - col_move + 1
+        matrix = jnp.zeros((extent, COL_TILE), f32)
+        for tap in range(TAP_COUNT):
+            taps = col_weights[tap : tap + 1, tile * COL_TILE : (tile + 1) * COL_TILE]
+            matrix = jnp.where(offsets == tap, taps, matrix)
+        col_mats[tile, 0:extent, :] = matrix.astype(bf16)
+
+    ext = rows + 2 * BLOCK
+    source_ids = lax.broadcasted_iota(jnp.int32, (ext, rows), 0)
+    target_ids = lax.broadcasted_iota(jnp.int32, (ext, rows), 1)
+    offsets = source_ids - target_ids - BLOCK - row_shift[0, 0] + 1
+    row_matrix = jnp.zeros((ext, rows), f32)
+    for tap in range(TAP_COUNT):
+        row_matrix = jnp.where(offsets == tap, row_weights[tap : tap + 1, :], row_matrix)
+    parts = []
+    rest = row_matrix
+    for _ in range(3):
+        part = rest.astype(bf16)
+        parts.append(part)
+        rest = rest - part.astype(f32)
+
+    exchange_wait(img_up, img_down)
+    row_warped = jnp.zeros((rows, width), f32)
+    for part in reversed(parts):
+        row_warped = row_warped + lax.dot_general(
+            part, img_ext[...], (((0,), (0,)), ((), ())), preferred_element_type=f32
+        )
+    row_warped = row_warped.astype(bf16)
+    for tile, (first, last) in enumerate(spans):
+        piece = jnp.dot(
+            row_warped[:, first:last], col_mats[tile, 0 : last - first, :], preferred_element_type=f32
+        ).astype(bf16)
+        warp_ext[1 : n + 1, :, tile * COL_TILE : (tile + 1) * COL_TILE] = piece.reshape(n, BLOCK, COL_TILE)
+
+    halo_up = remote(warp_ext.at[1], warp_ext.at[n + 1], halo_send.at[0], halo_recv.at[1], up)
+    halo_down = remote(warp_ext.at[n], warp_ext.at[0], halo_send.at[1], halo_recv.at[0], down)
+    exchange_start(halo_up, halo_down)
+
+    def window_copy(target):
+        return remote(
+            warp_ext.at[pl.ds(target, 3)], window.at[me], win_send.at[target], win_recv.at[me], {"sec": target}
+        )
+
+    def window_start(target):
+        @pl.when(target != me)
+        def _():
+            window_copy(target).start()
+
+    for target in range(1, n - 1):
+        window_start(target)
+    exchange_wait(halo_up, halo_down)
+    window_start(0)
+    window_start(n - 1)
+    window[me] = warp_ext[pl.ds(me, 3)]
+
+    half = BLOCK // 2
+    near = BLOCK + 2 * half
+    mid_rows = BLOCK + 2 * RADIUS
+
+    def statistics(step, carry):
+        sec = lax.rem(me + step, n)
+
+        @pl.when(sec != me)
+        def _():
+            remote(
+                warp_ext.at[pl.ds(0, 3)], window.at[sec], win_send.at[sec], win_recv.at[sec], {"sec": sec}
+            ).wait_recv()
+
+        values = window[sec].reshape(3 * BLOCK, width).astype(f32)[half : half + near]
+        field[sec] = values
+        average = cols_sum(rows_sum_from(values)) * (1.0 / cells)
+        square = cols_sum(rows_sum_from(values * values)) * (1.0 / cells)
+        mean[sec] = average
+        inv[sec] = lax.rsqrt(square - average * average + variance_bias)
+        ncc_sum[sec] = jnp.zeros((mid_rows, width), f32)
+        mean_sum[sec] = jnp.zeros((mid_rows, width), f32)
+        grad_acc[sec] = jnp.zeros((BLOCK, width), f32)
+        return carry
+
+    lax.fori_loop(0, n, statistics, 0)
+
+    row_ids = lax.broadcasted_iota(jnp.int32, (mid_rows, width), 0) + (z * rows + me * BLOCK - RADIUS)
+    inside = jnp.where((row_ids >= 0) & (row_ids < strips * rows), 1.0, 0.0).astype(f32)
+
+    for distance in range(1, PAIR_REACH + 1):
+
+        def one_pair(left, carry):
+            right = left + distance
+            weight = pair_on[left, distance - 1].astype(f32)
+            a, b = field[left], field[right]
+            mean_a, mean_b = mean[left], mean[right]
+            cov = cols_sum(rows_sum_from(a * b)) * (1.0 / cells) - mean_a * mean_b
+            scale = inv[left] * inv[right] * (inside * weight)
+            ncc = cov * scale
+            ncc_sum[left] += ncc
+            ncc_sum[right] += ncc
+            mean_sum[left] += scale * mean_b
+            mean_sum[right] += scale * mean_a
+            boxed = cols_sum(rows_sum_from(scale))
+            grad_acc[left] += boxed * b[half : half + BLOCK]
+            grad_acc[right] += boxed * a[half : half + BLOCK]
+            return carry
+
+        lax.fori_loop(0, n - distance, one_pair, 0)
+
+    def back_copy(sec):
+        return remote(
+            grad_send.at[sec], grad_ext.at[me + 1], back_send.at[sec], back_recv.at[me], {"sec": sec}
+        )
+
+    def finish(step, carry):
+        sec = lax.rem(me + 1 + step, n)
+        root = inv[sec]
+        g_twice = ncc_sum[sec] * root * root
+        h = mean_sum[sec] - mean[sec] * g_twice
+        boxed_h = cols_sum(rows_sum_from(h))
+        boxed_g = cols_sum(rows_sum_from(g_twice))
+        mid = field[sec, half : half + BLOCK, :]
+        total = (boxed_h + mid * boxed_g - grad_acc[sec]) * (1.0 / cells)
+        grad_send[sec] = total.astype(bf16)
+
+        @pl.when(sec != me)
+        def _():
+            back_copy(sec).start()
+
+        return carry
+
+    lax.fori_loop(0, n, finish, 0)
+    grad_ext[me + 1] = grad_send[me]
+
+    def back_wait(step, carry):
+        sec = lax.rem(me + step, n)
+        remote(
+            grad_send.at[sec], grad_ext.at[sec + 1], back_send.at[sec], back_recv.at[sec], {"sec": sec}
+        ).wait_recv()
+        return carry
+
+    lax.fori_loop(1, n, back_wait, 0)
+    edge_up = remote(grad_ext.at[1], grad_ext.at[n + 1], edge_send.at[0], edge_recv.at[1], up)
+    edge_down = remote(grad_ext.at[n], grad_ext.at[0], edge_send.at[1], edge_recv.at[0], down)
+    exchange_start(edge_up, edge_down)
+
+    def displace(block):
+        grads = grad_ext[pl.ds(block, 3)].reshape(3 * BLOCK, width).astype(f32)
+        warped = warp_ext[pl.ds(block, 3)].reshape(3 * BLOCK, width).astype(f32)
+        out_rows = pl.ds(pl.multiple_of(block * BLOCK, BLOCK), BLOCK)
+        grad_out[0, out_rows, :] = grads[BLOCK : 2 * BLOCK]
+        span = 3 * BLOCK
+        slope_rows = (pltpu.roll(warped, span - 1, 0) - pltpu.roll(warped, 1, 0))[half : half + near]
+        padded = with_zero_lanes(warped[half : half + near])
+        lanes = width + LANES
+        slope_cols = (pltpu.roll(padded, lanes - 1, 1) - pltpu.roll(padded, 1, 1))[:, :width]
+        near_grads = grads[half : half + near] * (-0.5 / 9.0)
+        for part, slope in enumerate((slope_rows, slope_cols)):
+            summed = rows_sum_centred(near_grads * slope)[half : half + BLOCK]
+            disp_out[part, 0, out_rows, :] = cols_sum(summed)
+
+    def displace_step(block, carry):
+        displace(block)
+        return carry
+
+    lax.fori_loop(1, n - 1, displace_step, 0)
+    exchange_wait(edge_up, edge_down)
+
+    def displace_end(step, carry):
+        displace(step * (n - 1))
+        return carry
+
+    lax.fori_loop(0, 2, displace_end, 0)
+
+    def drain(step, carry):
+        sec = lax.rem(me + step, n)
+        window_copy(sec).wait_send()
+        back_copy(sec).wait_send()
+        return carry
+
+    lax.fori_loop(1, n, drain, 0)
+
+
+def fused(n, strips, images, row_weights, row_shift, col_weights, col_shift, pair_on):
+    _, rows, width = images.shape
+    f32, bf16 = jnp.float32, jnp.bfloat16
+    mid_rows = BLOCK + 2 * RADIUS
+    vmem = pl.BlockSpec(memory_space=pltpu.VMEM)
+    smem = pl.BlockSpec(memory_space=pltpu.SMEM)
+    dma = pltpu.SemaphoreType.DMA
+    return pl.pallas_call(
+        functools.partial(align_kernel, n, strips),
+        out_shape=(
+            jax.ShapeDtypeStruct((1, rows, width), f32),
+            jax.ShapeDtypeStruct((2, 1, rows, width), f32),
+        ),
+        in_specs=[vmem, vmem, smem, vmem, smem, smem],
+        out_specs=(vmem, vmem),
+        scratch_shapes=[
+            pltpu.VMEM((rows + 2 * BLOCK, width), bf16),
+            pltpu.VMEM((width // COL_TILE, COL_TILE + 2 * LANES, COL_TILE), bf16),
+            pltpu.VMEM((n + 2, BLOCK, width), bf16),
+            pltpu.VMEM((n, 3, BLOCK, width), bf16),
+            pltpu.VMEM((n, 2 * BLOCK, width), f32),
+            pltpu.VMEM((n, mid_rows, width), f32),
+            pltpu.VMEM((n, mid_rows, width), f32),
+            pltpu.VMEM((n, mid_rows, width), f32),
+            pltpu.VMEM((n, mid_rows, width), f32),
+            pltpu.VMEM((n, BLOCK, width), f32),
+            pltpu.VMEM((n, BLOCK, width), bf16),
+            pltpu.VMEM((n + 2, BLOCK, width), bf16),
+            dma((2,)),
+            dma((2,)),
+            dma((2,)),
+            dma((2,)),
+            dma((n,)),
+            dma((n,)),
+            dma((n,)),
+            dma((n,)),
+            dma((2,)),
+            dma((2,)),
+        ],
+        compiler_params=pltpu.CompilerParams(
+            collective_id=0, has_side_effects=True, vmem_limit_bytes=40 * 1024 * 1024
+        ),
+    )(images[0], row_weights[0], row_shift, col_weights[0].astype(f32), col_shift, pair_on)
+
+
 def solution(mesh):
+    n, strips = mesh.shape["sec"], mesh.shape["strip"]
+
+    def step(images, *rest):
+        sections, rows, width = images.shape
+        if sections == 1 and rows == n * BLOCK and width % COL_TILE == 0:
+            return fused(n, strips, images, *rest)
+        return per_device(images, *rest)
+
     return jax.shard_map(
-        per_device,
+        step,
         mesh=mesh,
         in_specs=(
             P("sec", "strip", None),

time: 149 us -> 43.3 us (0.29)
  the two profiles are of different devices: /device:TPU:4 before, /device:TPU:0 now
where the time goes in v1:
time: 43.3 us; the launch traced here: 43.1 us
  Pallas kernels  37 us (85%)
  local copies, waits for them, and re-layouts  4.15 us (10%)
  between operations  1.96 us (5%)
    pallas_call x1, Pallas kernels, fused(): pl.pallas_call(functools.partial(align_kernel, n, strips), out_shape=(jax...  37 us
    unnamed x9, local copies, waits for them, and re-layouts  4.15 us

profile of v1, /device:TPU:0, one launch (start us, length us, event | category | flops | bytes accessed | tf_op | source)
XLA Modules:
  0.0 43.1 jit_solution(263538141471507472)
XLA Ops:
  0.6 0.0 copy-start.2
  1.9 0.8 %copy.8.pair_on = s32[8,3]{1,0:T(8,128)S(1)} copy(s32[8,3]{0,1:T(4,128)} %param.11) | data formatting | bytes 192 | tf_op args[5]
  2.7 0.0 copy-done.2
  2.7 0.0 copy-start.1
  2.7 0.7 %copy-done.1 = f32[1,4,128]{2,1,0:T(4,128)S(1)} copy-done((f32[1,4,128]{2,1,0:T(4,128)S(1)}, f32[1,4,128]{2,1,0:T(4,128)}, u32[]{:S(2)}) %copy-start.1) | copy-done | bytes 2072
  3.4 0.0 copy-start
  3.4 0.9 %copy-done = bf16[1,128,1024]{2,1,0:T(8,128)(2,1)S(1)} copy-done((bf16[1,128,1024]{2,1,0:T(8,128)(2,1)S(1)}, bf16[1,128,1024]{2,1,0:T(8,128)(2,1)}, u32[]{:S(2)}) %copy-start) | copy-done | bytes 262168
  4.3 37.0 %shard_map.77 = (f32[1,128,1024]{2,1,0:T(8,128)S(1)}, f32[2,1,128,1024]{3,2,1,0:T(8,128)S(1)}) custom-call(bf16[128,1024]{1,0:T(8,128)(2,1)S(1)} %bitcast.5, f32[4,128]{1,0:T(4,128)S(1)} %bitcast.6, s32[1,1]{1,0:T(1,128)S(6)} %copy.11.row_shift, f32[4,1024]{1,0:T(4,128)S(1)} %bitcast_convert_fusion.col_weights, s32[1]{0:T(128)S(6)} %copy.12.col_shift, ...), custom_call_target="tpu_custom_call" | custom-call | tf_op jit(solution)/shard_map/pallas_call | solution.py:510
  41.3 0.8 %copy.13 = f32[1,128,1024]{2,1,0:T(8,128)} copy(f32[1,128,1024]{2,1,0:T(8,128)S(1)} %get-tuple-element.4) | data formatting | bytes 1048576
  42.1 1.0 %copy.14 = f32[2,1,128,1024]{3,2,1,0:T(8,128)} copy(f32[2,1,128,1024]{3,2,1,0:T(8,128)S(1)} %get-tuple-element.5) | data formatting | bytes 2097152
  (1 shorter events, 0.0 us)
Async XLA Ops:
  0.6 2.1 %copy-start.2 = (bf16[1,4,1024]{2,1,0:T(4,128)(2,1)S(1)}, bf16[1,4,1024]{2,1,0:T(4,128)(2,1)}, u32[]{:S(2)}) copy-start(bf16[1,4,1024]{2,1,0:T(4,128)(2,1)} %param.9) | copy-start | bytes 24580
  2.7 0.7 %copy-start.1 = (f32[1,4,128]{2,1,0:T(4,128)S(1)}, f32[1,4,128]{2,1,0:T(4,128)}, u32[]{:S(2)}) copy-start(f32[1,4,128]{2,1,0:T(4,128)} %param.7) | copy-start | bytes 6148
  3.4 0.9 %copy-start = (bf16[1,128,1024]{2,1,0:T(8,128)(2,1)S(1)}, bf16[1,128,1024]{2,1,0:T(8,128)(2,1)}, u32[]{:S(2)}) copy-start(bf16[1,128,1024]{2,1,0:T(8,128)(2,1)} %param.6) | copy-start | bytes 786436

commit v2 on v1

--- a/solution.py
+++ b/solution.py
@@ -174,6 +174,7 @@
 
 MESH = pl.DeviceIdType.MESH
 BLOCK = 16
+HALF_ROWS = BLOCK // 2
 LANES = 128
 COL_TILE = 256
 
@@ -202,6 +203,13 @@
     t = x + pltpu.roll(x, m - 1, 1) + pltpu.roll(x, 1, 1)
     t = t + pltpu.roll(t, m - 3, 1) + pltpu.roll(t, 3, 1)
     return t[:, :width]
+
+
+def halves_to_rows(x):
+    x = x.astype(jnp.float32)
+    count, _, half = x.shape
+    rows = jnp.concatenate([x[:, :HALF_ROWS], x[:, HALF_ROWS:]], axis=2)
+    return rows.reshape(count * HALF_ROWS, 2 * half)
 
 
 def align_kernel(
@@ -213,11 +221,12 @@
     col_weights,
     col_shift,
     pair_on,
-    grad_out,
-    disp_out,
+    grad_done,
+    warp_done,
+    grad_ext,
+    warp_ext,
     img_ext,
     col_mats,
-    warp_ext,
     window,
     field,
     mean,
@@ -226,7 +235,6 @@
     mean_sum,
     grad_acc,
     grad_send,
-    grad_ext,
     img_send,
     img_recv,
     halo_send,
@@ -248,6 +256,7 @@
     down = {"strip": z + 1}
     cells = float((2 * RADIUS + 1) ** 2)
 
+
     def remote(src, dst, send, recv, where):
         return pltpu.make_async_remote_copy(
             src_ref=src, dst_ref=dst, send_sem=send, recv_sem=recv, device_id=where, device_id_type=MESH
@@ -298,23 +307,26 @@
 
     exchange_start(img_up, img_down)
     zero_block = jnp.zeros((BLOCK, width), bf16)
+    zero_half = jnp.zeros((BLOCK, width // 2), bf16)
+    bottom = 2 * n + 1
 
     @pl.when(jnp.logical_not(has_up))
     def _():
         img_ext[0:BLOCK] = zero_block
-        warp_ext[0] = zero_block
+        warp_ext[0] = zero_half
         grad_ext[0] = zero_block
 
     @pl.when(jnp.logical_not(has_down))
     def _():
         img_ext[rows + BLOCK : rows + 2 * BLOCK] = zero_block
-        warp_ext[n + 1] = zero_block
+        warp_ext[bottom] = zero_half
         grad_ext[n + 1] = zero_block
 
-    img_ext[BLOCK : rows + BLOCK] = images[...]
     col_move = col_shift[0]
+    all_taps = col_weights[...].astype(f32)
     spans = []
-    for tile in range(width // COL_TILE):
+    tiles = width // COL_TILE
+    for tile in range(tiles):
         first = max(0, tile * COL_TILE - LANES)
         last = min(width, (tile + 1) * COL_TILE + LANES)
         spans.append((first, last))
@@ -324,7 +336,7 @@
         offsets = row_ids - col_ids - col_move + 1
         matrix = jnp.zeros((extent, COL_TILE), f32)
         for tap in range(TAP_COUNT):
-            taps = col_weights[tap : tap + 1, tile * COL_TILE : (tile + 1) * COL_TILE]
+            taps = all_taps[tap : tap + 1, tile * COL_TILE : (tile + 1) * COL_TILE]
             matrix = jnp.where(offsets == tap, taps, matrix)
         col_mats[tile, 0:extent, :] = matrix.astype(bf16)
 
@@ -342,6 +354,7 @@
         parts.append(part)
         rest = rest - part.astype(f32)
 
+    img_ext[BLOCK : rows + BLOCK] = images[...]
     exchange_wait(img_up, img_down)
     row_warped = jnp.zeros((rows, width), f32)
     for part in reversed(parts):
@@ -349,47 +362,79 @@
             part, img_ext[...], (((0,), (0,)), ((), ())), preferred_element_type=f32
         )
     row_warped = row_warped.astype(bf16)
-    for tile, (first, last) in enumerate(spans):
+
+    def warped_tile(tile):
+        first, last = spans[tile]
         piece = jnp.dot(
             row_warped[:, first:last], col_mats[tile, 0 : last - first, :], preferred_element_type=f32
-        ).astype(bf16)
-        warp_ext[1 : n + 1, :, tile * COL_TILE : (tile + 1) * COL_TILE] = piece.reshape(n, BLOCK, COL_TILE)
-
-    halo_up = remote(warp_ext.at[1], warp_ext.at[n + 1], halo_send.at[0], halo_recv.at[1], up)
-    halo_down = remote(warp_ext.at[n], warp_ext.at[0], halo_send.at[1], halo_recv.at[0], down)
+        )
+        return piece.reshape(2 * n, HALF_ROWS, COL_TILE)
+
+    for tile in range(tiles // 2):
+        both = jnp.concatenate([warped_tile(tile), warped_tile(tile + tiles // 2)], axis=1)
+        warp_ext[1:bottom, :, tile * COL_TILE : (tile + 1) * COL_TILE] = both.astype(bf16)
+
+    halo_up = remote(warp_ext.at[1], warp_ext.at[bottom], halo_send.at[0], halo_recv.at[1], up)
+    halo_down = remote(warp_ext.at[bottom - 1], warp_ext.at[0], halo_send.at[1], halo_recv.at[0], down)
     exchange_start(halo_up, halo_down)
 
     def window_copy(target):
         return remote(
-            warp_ext.at[pl.ds(target, 3)], window.at[me], win_send.at[target], win_recv.at[me], {"sec": target}
-        )
-
-    def window_start(target):
-        @pl.when(target != me)
+            warp_ext.at[pl.ds(2 * target, 4)], window.at[me], win_send.at[target], win_recv.at[me], {"sec": target}
+        )
+
+    def send_inner(step, carry):
+        target = lax.rem(me + n - step, n)
+
+        @pl.when((target > 0) & (target < n - 1))
         def _():
             window_copy(target).start()
 
-    for target in range(1, n - 1):
-        window_start(target)
+        return carry
+
+    def send_outer(step, carry):
+        target = lax.rem(me + n - step, n)
+
+        @pl.when((target == 0) | (target == n - 1))
+        def _():
+            window_copy(target).start()
+
+        return carry
+
+    lax.fori_loop(1, n, send_inner, 0)
     exchange_wait(halo_up, halo_down)
-    window_start(0)
-    window_start(n - 1)
-    window[me] = warp_ext[pl.ds(me, 3)]
-
-    half = BLOCK // 2
-    near = BLOCK + 2 * half
+    lax.fori_loop(1, n, send_outer, 0)
+    window[me] = warp_ext[pl.ds(2 * me, 4)]
+
     mid_rows = BLOCK + 2 * RADIUS
-
-    def statistics(step, carry):
+    row_ids = lax.broadcasted_iota(jnp.int32, (mid_rows, width), 0) + (z * rows + me * BLOCK - RADIUS)
+    inside = jnp.where((row_ids >= 0) & (row_ids < strips * rows), 1.0, 0.0).astype(f32)
+
+    def one_pair(left, right, distance):
+        weight = pair_on[left, distance - 1].astype(f32)
+        a, b = field[left], field[right]
+        mean_a, mean_b = mean[left], mean[right]
+        cov = cols_sum(rows_sum_from(a * b)) * (1.0 / cells) - mean_a * mean_b
+        scale = inv[left] * inv[right] * (inside * weight)
+        ncc = cov * scale
+        ncc_sum[left] += ncc
+        ncc_sum[right] += ncc
+        mean_sum[left] += scale * mean_b
+        mean_sum[right] += scale * mean_a
+        boxed = cols_sum(rows_sum_from(scale))
+        grad_acc[left] += boxed * b[HALF_ROWS : HALF_ROWS + BLOCK]
+        grad_acc[right] += boxed * a[HALF_ROWS : HALF_ROWS + BLOCK]
+
+    def meet(step, carry):
         sec = lax.rem(me + step, n)
 
-        @pl.when(sec != me)
+        @pl.when(step > 0)
         def _():
             remote(
-                warp_ext.at[pl.ds(0, 3)], window.at[sec], win_send.at[sec], win_recv.at[sec], {"sec": sec}
+                warp_ext.at[pl.ds(0, 4)], window.at[sec], win_send.at[sec], win_recv.at[sec], {"sec": sec}
             ).wait_recv()
 
-        values = window[sec].reshape(3 * BLOCK, width).astype(f32)[half : half + near]
+        values = halves_to_rows(window[sec])
         field[sec] = values
         average = cols_sum(rows_sum_from(values)) * (1.0 / cells)
         square = cols_sum(rows_sum_from(values * values)) * (1.0 / cells)
@@ -398,33 +443,22 @@
         ncc_sum[sec] = jnp.zeros((mid_rows, width), f32)
         mean_sum[sec] = jnp.zeros((mid_rows, width), f32)
         grad_acc[sec] = jnp.zeros((BLOCK, width), f32)
+
+        def with_earlier(distance, carry):
+            @pl.when((sec >= distance) & (lax.rem(sec - distance - me + 2 * n, n) < step))
+            def _():
+                one_pair(lax.rem(sec - distance + n, n), sec, distance)
+
+            @pl.when((sec + distance < n) & (lax.rem(sec + distance - me + 2 * n, n) < step))
+            def _():
+                one_pair(sec, lax.rem(sec + distance, n), distance)
+
+            return carry
+
+        lax.fori_loop(1, PAIR_REACH + 1, with_earlier, 0)
         return carry
 
-    lax.fori_loop(0, n, statistics, 0)
-
-    row_ids = lax.broadcasted_iota(jnp.int32, (mid_rows, width), 0) + (z * rows + me * BLOCK - RADIUS)
-    inside = jnp.where((row_ids >= 0) & (row_ids < strips * rows), 1.0, 0.0).astype(f32)
-
-    for distance in range(1, PAIR_REACH + 1):
-
-        def one_pair(left, carry):
-            right = left + distance
-            weight = pair_on[left, distance - 1].astype(f32)
-            a, b = field[left], field[right]
-            mean_a, mean_b = mean[left], mean[right]
-            cov = cols_sum(rows_sum_from(a * b)) * (1.0 / cells) - mean_a * mean_b
-            scale = inv[left] * inv[right] * (inside * weight)
-            ncc = cov * scale
-            ncc_sum[left] += ncc
-            ncc_sum[right] += ncc
-            mean_sum[left] += scale * mean_b
-            mean_sum[right] += scale * mean_a
-            boxed = cols_sum(rows_sum_from(scale))
-            grad_acc[left] += boxed * b[half : half + BLOCK]
-            grad_acc[right] += boxed * a[half : half + BLOCK]
-            return carry
-
-        lax.fori_loop(0, n - distance, one_pair, 0)
+    lax.fori_loop(0, n, meet, 0)
 
     def back_copy(sec):
         return remote(
@@ -438,7 +472,7 @@
         h = mean_sum[sec] - mean[sec] * g_twice
         boxed_h = cols_sum(rows_sum_from(h))
         boxed_g = cols_sum(rows_sum_from(g_twice))
-        mid = field[sec, half : half + BLOCK, :]
+        mid = field[sec, HALF_ROWS : HALF_ROWS + BLOCK, :]
         total = (boxed_h + mid * boxed_g - grad_acc[sec]) * (1.0 / cells)
         grad_send[sec] = total.astype(bf16)
 
@@ -451,53 +485,66 @@
     lax.fori_loop(0, n, finish, 0)
     grad_ext[me + 1] = grad_send[me]
 
-    def back_wait(step, carry):
+    def drain(step, carry):
         sec = lax.rem(me + step, n)
-        remote(
-            grad_send.at[sec], grad_ext.at[sec + 1], back_send.at[sec], back_recv.at[sec], {"sec": sec}
-        ).wait_recv()
+
+        @pl.when(step > 0)
+        def _():
+            window_copy(sec).wait_send()
+            back_copy(sec).wait_send()
+            remote(
+                grad_send.at[sec], grad_ext.at[sec + 1], back_send.at[sec], back_recv.at[sec], {"sec": sec}
+            ).wait_recv()
+
         return carry
 
-    lax.fori_loop(1, n, back_wait, 0)
+    lax.fori_loop(0, n, drain, 0)
+
     edge_up = remote(grad_ext.at[1], grad_ext.at[n + 1], edge_send.at[0], edge_recv.at[1], up)
     edge_down = remote(grad_ext.at[n], grad_ext.at[0], edge_send.at[1], edge_recv.at[0], down)
     exchange_start(edge_up, edge_down)
-
-    def displace(block):
+    exchange_wait(edge_up, edge_down)
+    grad_done[...] = grad_ext[...]
+    warp_done[...] = warp_ext[...]
+
+
+def displace_kernel(n, grad_ext, warp_ext, grad_out, disp_out, grad_rows, disp_rows, grad_sems, disp_sems):
+    _, rows, width = grad_rows.shape
+    f32 = jnp.float32
+
+    def copies(block):
+        out_rows = pl.ds(pl.multiple_of(block * BLOCK, BLOCK), BLOCK)
+        return [
+            pltpu.make_async_copy(grad_rows.at[:, out_rows], grad_out.at[:, out_rows], grad_sems.at[block]),
+            pltpu.make_async_copy(disp_rows.at[:, :, out_rows], disp_out.at[:, :, out_rows], disp_sems.at[block]),
+        ]
+
+    def displace(block, carry):
+        near = BLOCK + 2 * HALF_ROWS
         grads = grad_ext[pl.ds(block, 3)].reshape(3 * BLOCK, width).astype(f32)
-        warped = warp_ext[pl.ds(block, 3)].reshape(3 * BLOCK, width).astype(f32)
+        warped = halves_to_rows(warp_ext[pl.ds(2 * block, 4)])
         out_rows = pl.ds(pl.multiple_of(block * BLOCK, BLOCK), BLOCK)
-        grad_out[0, out_rows, :] = grads[BLOCK : 2 * BLOCK]
-        span = 3 * BLOCK
-        slope_rows = (pltpu.roll(warped, span - 1, 0) - pltpu.roll(warped, 1, 0))[half : half + near]
-        padded = with_zero_lanes(warped[half : half + near])
+        grad_rows[0, out_rows, :] = grads[BLOCK : 2 * BLOCK]
+        slope_rows = pltpu.roll(warped, near - 1, 0) - pltpu.roll(warped, 1, 0)
+        padded = with_zero_lanes(warped)
         lanes = width + LANES
         slope_cols = (pltpu.roll(padded, lanes - 1, 1) - pltpu.roll(padded, 1, 1))[:, :width]
-        near_grads = grads[half : half + near] * (-0.5 / 9.0)
+        near_grads = grads[HALF_ROWS : HALF_ROWS + near] * (-0.5 / 9.0)
         for part, slope in enumerate((slope_rows, slope_cols)):
-            summed = rows_sum_centred(near_grads * slope)[half : half + BLOCK]
-            disp_out[part, 0, out_rows, :] = cols_sum(summed)
-
-    def displace_step(block, carry):
-        displace(block)
+            summed = rows_sum_centred(near_grads * slope)[HALF_ROWS : HALF_ROWS + BLOCK]
+            disp_rows[part, 0, out_rows, :] = cols_sum(summed)
+        for copy in copies(block):
+            copy.start()
         return carry
 
-    lax.fori_loop(1, n - 1, displace_step, 0)
-    exchange_wait(edge_up, edge_down)
-
-    def displace_end(step, carry):
-        displace(step * (n - 1))
+    lax.fori_loop(0, n, displace, 0)
+
+    def drain(block, carry):
+        for copy in copies(block):
+            copy.wait()
         return carry
 
-    lax.fori_loop(0, 2, displace_end, 0)
-
-    def drain(step, carry):
-        sec = lax.rem(me + step, n)
-        window_copy(sec).wait_send()
-        back_copy(sec).wait_send()
-        return carry
-
-    lax.fori_loop(1, n, drain, 0)
+    lax.fori_loop(0, n, drain, 0)
 
 
 def fused(n, strips, images, row_weights, row_shift, col_weights, col_shift, pair_on):
@@ -506,20 +553,22 @@
     mid_rows = BLOCK + 2 * RADIUS
     vmem = pl.BlockSpec(memory_space=pltpu.VMEM)
     smem = pl.BlockSpec(memory_space=pltpu.SMEM)
+    where = pl.BlockSpec(memory_space=pltpu.HBM)
     dma = pltpu.SemaphoreType.DMA
-    return pl.pallas_call(
+    grad_ext, warp_ext = pl.pallas_call(
         functools.partial(align_kernel, n, strips),
         out_shape=(
-            jax.ShapeDtypeStruct((1, rows, width), f32),
-            jax.ShapeDtypeStruct((2, 1, rows, width), f32),
+            jax.ShapeDtypeStruct((n + 2, BLOCK, width), bf16),
+            jax.ShapeDtypeStruct((2 * n + 2, BLOCK, width // 2), bf16),
         ),
         in_specs=[vmem, vmem, smem, vmem, smem, smem],
         out_specs=(vmem, vmem),
         scratch_shapes=[
+            pltpu.VMEM((n + 2, BLOCK, width), bf16),
+            pltpu.VMEM((2 * n + 2, BLOCK, width // 2), bf16),
             pltpu.VMEM((rows + 2 * BLOCK, width), bf16),
             pltpu.VMEM((width // COL_TILE, COL_TILE + 2 * LANES, COL_TILE), bf16),
-            pltpu.VMEM((n + 2, BLOCK, width), bf16),
-            pltpu.VMEM((n, 3, BLOCK, width), bf16),
+            pltpu.VMEM((n, 4, BLOCK, width // 2), bf16),
             pltpu.VMEM((n, 2 * BLOCK, width), f32),
             pltpu.VMEM((n, mid_rows, width), f32),
             pltpu.VMEM((n, mid_rows, width), f32),
@@ -527,7 +576,6 @@
             pltpu.VMEM((n, mid_rows, width), f32),
             pltpu.VMEM((n, BLOCK, width), f32),
             pltpu.VMEM((n, BLOCK, width), bf16),
-            pltpu.VMEM((n + 2, BLOCK, width), bf16),
             dma((2,)),
             dma((2,)),
             dma((2,)),
@@ -536,13 +584,29 @@
             dma((n,)),
             dma((n,)),
             dma((n,)),
-            dma((2,)),
+            dma((n,)),
             dma((2,)),
         ],
         compiler_params=pltpu.CompilerParams(
             collective_id=0, has_side_effects=True, vmem_limit_bytes=40 * 1024 * 1024
         ),
-    )(images[0], row_weights[0], row_shift, col_weights[0].astype(f32), col_shift, pair_on)
+    )(images[0], row_weights[0], row_shift, col_weights[0], col_shift, pair_on)
+    return pl.pallas_call(
+        functools.partial(displace_kernel, n),
+        out_shape=(
+            jax.ShapeDtypeStruct((1, rows, width), f32),
+            jax.ShapeDtypeStruct((2, 1, rows, width), f32),
+        ),
+        in_specs=[vmem, vmem],
+        out_specs=(where, where),
+        scratch_shapes=[
+            pltpu.VMEM((1, rows, width), f32),
+            pltpu.VMEM((2, 1, rows, width), f32),
+            dma((n,)),
+            dma((n,)),
+        ],
+        compiler_params=pltpu.CompilerParams(vmem_limit_bytes=40 * 1024 * 1024),
+    )(grad_ext, warp_ext)
 
 
 def solution(mesh):
@@ -550,7 +614,7 @@
 
     def step(images, *rest):
         sections, rows, width = images.shape
-        if sections == 1 and rows == n * BLOCK and width % COL_TILE == 0:
+        if sections == 1 and rows == n * BLOCK and width % (2 * COL_TILE) == 0:
             return fused(n, strips, images, *rest)
         return per_device(images, *rest)
 

time: 43.3 us -> 41.3 us (0.954)
  local copies, waits for them, and re-layouts: 4.15 us -> 1.72 us
    pallas_call x0 -> x1, Pallas kernels: none -> 4.04 us  [fused(): pl.pallas_call(functools.partial(displace_kernel, n), out_shape=(jax.Shap...]
    pallas_call x1, Pallas kernels: 37 us -> 33.3 us  [fused(): pl.pallas_call(functools.partial(align_kernel, n, strips), out_shape=(jax...]
    unnamed x9 -> x7, local copies, waits for them, and re-layouts: 4.15 us -> 1.72 us
where the time goes in v2:
time: 41.3 us; the launch traced here: 41 us
  Pallas kernels  37.4 us (91%)
  between operations  1.96 us (5%)
  local copies, waits for them, and re-layouts  1.72 us (4%)
    pallas_call x1, Pallas kernels, fused(): pl.pallas_call(functools.partial(align_kernel, n, strips), out_shape=(jax...  33.3 us
    pallas_call x1, Pallas kernels, fused(): pl.pallas_call(functools.partial(displace_kernel, n), out_shape=(jax.Shap...  4.04 us
    unnamed x7, local copies, waits for them, and re-layouts  1.72 us

profile of v2, /device:TPU:0, one launch (start us, length us, event | category | flops | bytes accessed | tf_op | source)
XLA Modules:
  0.0 41.0 jit_solution(13568016978247587162)
XLA Ops:
  0.6 0.0 copy-start.1
  1.9 0.0 copy-start.2
  2.0 0.8 %copy.8.pair_on = s32[8,3]{1,0:T(8,128)S(1)} copy(s32[8,3]{0,1:T(4,128)} %param.11) | data formatting | bytes 192 | tf_op args[5]
  2.7 0.0 copy-done.1
  2.7 0.0 copy-done.2
  2.7 0.0 copy-start
  2.7 0.9 %copy-done = bf16[1,128,1024]{2,1,0:T(8,128)(2,1)S(1)} copy-done((bf16[1,128,1024]{2,1,0:T(8,128)(2,1)S(1)}, bf16[1,128,1024]{2,1,0:T(8,128)(2,1)}, u32[]{:S(2)}) %copy-start) | copy-done | bytes 262168
  3.7 33.3 %shard_map.77 = (bf16[10,16,1024]{2,1,0:T(8,128)(2,1)S(1)}, bf16[18,16,512]{2,1,0:T(8,128)(2,1)S(1)}) custom-call(bf16[128,1024]{1,0:T(8,128)(2,1)S(1)} %bitcast.3, f32[4,128]{1,0:T(4,128)S(1)} %bitcast.5, s32[1,1]{1,0:T(1,128)S(6)} %copy.9.row_shift, bf16[4,1024]{1,0:T(4,128)(2,1)S(1)} %bitcast.4, s32[1]{0:T(128)S(6)} %copy.10.col_shift, ...), custom_call_target="tpu_custom_call" | custom-call | tf_op jit(solution)/shard_map/pallas_call | solution.py:558
  37.0 4.0 %shard_map.78 = (f32[1,128,1024]{2,1,0:T(8,128)}, f32[2,1,128,1024]{3,2,1,0:T(8,128)}) custom-call(bf16[10,16,1024]{2,1,0:T(8,128)(2,1)S(1)} %get-tuple-element.4.grad_ext, bf16[18,16,512]{2,1,0:T(8,128)(2,1)S(1)} %get-tuple-element.5.warp_ext), custom_call_target="tpu_custom_call" | custom-call | tf_op jit(solution)/shard_map/pallas_call | solution.py:594
Async XLA Ops:
  0.6 2.1 %copy-start.1 = (bf16[1,4,1024]{2,1,0:T(4,128)(2,1)S(1)}, bf16[1,4,1024]{2,1,0:T(4,128)(2,1)}, u32[]{:S(2)}) copy-start(bf16[1,4,1024]{2,1,0:T(4,128)(2,1)} %param.9) | copy-start | bytes 24580
  1.9 0.8 %copy-start.2 = (f32[1,4,128]{2,1,0:T(4,128)S(1)}, f32[1,4,128]{2,1,0:T(4,128)}, u32[]{:S(2)}) copy-start(f32[1,4,128]{2,1,0:T(4,128)} %param.7) | copy-start | bytes 6148
  2.7 1.0 %copy-start = (bf16[1,128,1024]{2,1,0:T(8,128)(2,1)S(1)}, bf16[1,128,1024]{2,1,0:T(8,128)(2,1)}, u32[]{:S(2)}) copy-start(bf16[1,128,1024]{2,1,0:T(8,128)(2,1)} %param.6) | copy-start | bytes 786436

commit v3 on v2

--- a/solution.py
+++ b/solution.py
@@ -411,7 +411,7 @@
     inside = jnp.where((row_ids >= 0) & (row_ids < strips * rows), 1.0, 0.0).astype(f32)
 
     def one_pair(left, right, distance):
-        weight = pair_on[left, distance - 1].astype(f32)
+        weight = pair_on[distance - 1, left].astype(f32)
         a, b = field[left], field[right]
         mean_a, mean_b = mean[left], mean[right]
         cov = cols_sum(rows_sum_from(a * b)) * (1.0 / cells) - mean_a * mean_b
@@ -508,43 +508,50 @@
     warp_done[...] = warp_ext[...]
 
 
-def displace_kernel(n, grad_ext, warp_ext, grad_out, disp_out, grad_rows, disp_rows, grad_sems, disp_sems):
+def displace_kernel(n, grad_ext, warp_ext, grad_out, disp_out, grad_rows, disp_rows, terms, sems):
     _, rows, width = grad_rows.shape
-    f32 = jnp.float32
-
-    def copies(block):
-        out_rows = pl.ds(pl.multiple_of(block * BLOCK, BLOCK), BLOCK)
-        return [
-            pltpu.make_async_copy(grad_rows.at[:, out_rows], grad_out.at[:, out_rows], grad_sems.at[block]),
-            pltpu.make_async_copy(disp_rows.at[:, :, out_rows], disp_out.at[:, :, out_rows], disp_sems.at[block]),
-        ]
-
-    def displace(block, carry):
-        near = BLOCK + 2 * HALF_ROWS
-        grads = grad_ext[pl.ds(block, 3)].reshape(3 * BLOCK, width).astype(f32)
-        warped = halves_to_rows(warp_ext[pl.ds(2 * block, 4)])
-        out_rows = pl.ds(pl.multiple_of(block * BLOCK, BLOCK), BLOCK)
-        grad_rows[0, out_rows, :] = grads[BLOCK : 2 * BLOCK]
-        slope_rows = pltpu.roll(warped, near - 1, 0) - pltpu.roll(warped, 1, 0)
-        padded = with_zero_lanes(warped)
-        lanes = width + LANES
-        slope_cols = (pltpu.roll(padded, lanes - 1, 1) - pltpu.roll(padded, 1, 1))[:, :width]
-        near_grads = grads[HALF_ROWS : HALF_ROWS + near] * (-0.5 / 9.0)
-        for part, slope in enumerate((slope_rows, slope_cols)):
-            summed = rows_sum_centred(near_grads * slope)[HALF_ROWS : HALF_ROWS + BLOCK]
-            disp_rows[part, 0, out_rows, :] = cols_sum(summed)
-        for copy in copies(block):
-            copy.start()
-        return carry
-
-    lax.fori_loop(0, n, displace, 0)
-
-    def drain(block, carry):
-        for copy in copies(block):
-            copy.wait()
-        return carry
-
-    lax.fori_loop(0, n, drain, 0)
+    f32, bf16 = jnp.float32, jnp.bfloat16
+    grads = grad_ext[...].reshape((n + 2) * BLOCK, width).astype(f32)
+    grad_rows[0] = grads[BLOCK : BLOCK + rows]
+    grad_copy = pltpu.make_async_copy(grad_rows, grad_out, sems.at[2])
+    grad_copy.start()
+    near = rows + 2 * HALF_ROWS
+    near_grads = grads[HALF_ROWS : HALF_ROWS + near] * (-0.5 / 9.0)
+    warped = halves_to_rows(warp_ext[...])
+    slope_rows = pltpu.roll(warped, near - 1, 0) - pltpu.roll(warped, 1, 0)
+    padded = with_zero_lanes(warped)
+    lanes = width + LANES
+    slope_cols = (pltpu.roll(padded, lanes - 1, 1) - pltpu.roll(padded, 1, 1))[:, :width]
+
+    out_ids = lax.broadcasted_iota(jnp.int32, (rows, near), 0)
+    in_ids = lax.broadcasted_iota(jnp.int32, (rows, near), 1)
+    row_band = jnp.where(jnp.abs(in_ids - out_ids - HALF_ROWS) <= RADIUS, 1.0, 0.0).astype(bf16)
+    in_ids = lax.broadcasted_iota(jnp.int32, (COL_TILE + 2 * LANES, COL_TILE), 0)
+    out_ids = lax.broadcasted_iota(jnp.int32, (COL_TILE + 2 * LANES, COL_TILE), 1)
+    col_band = jnp.where(jnp.abs(in_ids - out_ids - LANES) <= RADIUS, 1.0, 0.0).astype(bf16)
+
+    def halves(x):
+        top = x.astype(bf16)
+        return top, (x - top.astype(f32)).astype(bf16)
+
+    for part, slope in enumerate((slope_rows, slope_cols)):
+        top, rest = halves(near_grads * slope)
+        summed = jnp.dot(row_band, rest, preferred_element_type=f32)
+        summed = summed + jnp.dot(row_band, top, preferred_element_type=f32)
+        top, rest = halves(summed)
+        terms[0:rows] = top
+        terms[rows : 2 * rows] = rest
+        for tile in range(width // COL_TILE):
+            base = tile * COL_TILE - LANES
+            first = max(0, base)
+            last = min(width, (tile + 1) * COL_TILE + LANES)
+            boxed = jnp.dot(terms[:, first:last], col_band[first - base : last - base], preferred_element_type=f32)
+            disp_rows[part, 0, :, tile * COL_TILE : (tile + 1) * COL_TILE] = boxed[:rows] + boxed[rows:]
+        pltpu.make_async_copy(disp_rows.at[part], disp_out.at[part], sems.at[part]).start()
+
+    for part in range(2):
+        pltpu.make_async_copy(disp_rows.at[part], disp_out.at[part], sems.at[part]).wait()
+    grad_copy.wait()
 
 
 def fused(n, strips, images, row_weights, row_shift, col_weights, col_shift, pair_on):
@@ -590,7 +597,7 @@
         compiler_params=pltpu.CompilerParams(
             collective_id=0, has_side_effects=True, vmem_limit_bytes=40 * 1024 * 1024
         ),
-    )(images[0], row_weights[0], row_shift, col_weights[0], col_shift, pair_on)
+    )(images[0], row_weights[0], row_shift, col_weights[0], col_shift, pair_on.T)
     return pl.pallas_call(
         functools.partial(displace_kernel, n),
         out_shape=(
@@ -602,8 +609,8 @@
         scratch_shapes=[
             pltpu.VMEM((1, rows, width), f32),
             pltpu.VMEM((2, 1, rows, width), f32),
-            dma((n,)),
-            dma((n,)),
+            pltpu.VMEM((2 * rows, width), bf16),
+            dma((3,)),
         ],
         compiler_params=pltpu.CompilerParams(vmem_limit_bytes=40 * 1024 * 1024),
     )(grad_ext, warp_ext)

time: 41.3 us -> 40 us (0.969)
  Pallas kernels: 37.4 us -> 35.5 us
  local copies, waits for them, and re-layouts: 1.72 us -> 2.3 us
    pallas_call x1, Pallas kernels: 4.04 us -> 2.22 us  [fused(): pl.pallas_call(functools.partial(displace_kernel, n), out_shape=(jax.Shap...]
    unnamed x7 -> x8, local copies, waits for them, and re-layouts: 1.72 us -> 2.3 us
where the time goes in v3:
time: 40 us; the launch traced here: 39.8 us
  Pallas kernels  35.5 us (89%)
  local copies, waits for them, and re-layouts  2.3 us (6%)
  between operations  1.97 us (5%)
    pallas_call x1, Pallas kernels, fused(): pl.pallas_call(functools.partial(align_kernel, n, strips), out_shape=(jax...  33.3 us
    unnamed x8, local copies, waits for them, and re-layouts  2.3 us
    pallas_call x1, Pallas kernels, fused(): pl.pallas_call(functools.partial(displace_kernel, n), out_shape=(jax.Shap...  2.22 us

profile of v3, /device:TPU:0, one launch (start us, length us, event | category | flops | bytes accessed | tf_op | source)
XLA Modules:
  0.0 39.8 jit_solution(16982879885927341448)
XLA Ops:
  0.6 0.0 copy-start.1
  1.9 0.0 copy-start.2
  2.0 0.0 copy-done.1
  2.0 0.7 %copy-done.2 = f32[1,4,128]{2,1,0:T(4,128)S(1)} copy-done((f32[1,4,128]{2,1,0:T(4,128)S(1)}, f32[1,4,128]{2,1,0:T(4,128)}, u32[]{:S(2)}) %copy-start.2) | copy-done | bytes 2072
  2.6 0.0 copy-start
  2.6 0.9 %copy-done = bf16[1,128,1024]{2,1,0:T(8,128)(2,1)S(1)} copy-done((bf16[1,128,1024]{2,1,0:T(8,128)(2,1)S(1)}, bf16[1,128,1024]{2,1,0:T(8,128)(2,1)}, u32[]{:S(2)}) %copy-start) | copy-done | bytes 262168
  3.6 0.0 copy-start.3
  3.6 0.7 %copy-done.3 = s32[8,3]{0,1:T(4,128)S(1)} copy-done((s32[8,3]{0,1:T(4,128)S(1)}, s32[8,3]{0,1:T(4,128)}, u32[]{:S(2)}) %copy-start.3) | copy-done | bytes 120
  4.3 33.3 %shard_map.77 = (bf16[10,16,1024]{2,1,0:T(8,128)(2,1)S(1)}, bf16[18,16,512]{2,1,0:T(8,128)(2,1)S(1)}) custom-call(bf16[128,1024]{1,0:T(8,128)(2,1)S(1)} %bitcast.4, f32[4,128]{1,0:T(4,128)S(1)} %bitcast.6, s32[1,1]{1,0:T(1,128)S(6)} %copy.8.row_shift, bf16[4,1024]{1,0:T(4,128)(2,1)S(1)} %bitcast.5, s32[1]{0:T(128)S(6)} %copy.9.col_shift, s32[3,8]{1,0:T(4,128)S(1)} %bitcast.7), custom_call_target="tpu_custom_call" | custom-call | tf_op jit(solution)/shard_map/pallas_call | solution.py:565
  37.5 2.2 %shard_map.78 = (f32[1,128,1024]{2,1,0:T(8,128)}, f32[2,1,128,1024]{3,2,1,0:T(8,128)}) custom-call(bf16[10,16,1024]{2,1,0:T(8,128)(2,1)S(1)} %get-tuple-element.4.grad_ext, bf16[18,16,512]{2,1,0:T(8,128)(2,1)S(1)} %get-tuple-element.5.warp_ext), custom_call_target="tpu_custom_call" | custom-call | tf_op jit(solution)/shard_map/pallas_call | solution.py:601
Async XLA Ops:
  0.6 1.3 %copy-start.1 = (bf16[1,4,1024]{2,1,0:T(4,128)(2,1)S(1)}, bf16[1,4,1024]{2,1,0:T(4,128)(2,1)}, u32[]{:S(2)}) copy-start(bf16[1,4,1024]{2,1,0:T(4,128)(2,1)} %param.9) | copy-start | bytes 24580
  1.9 0.7 %copy-start.2 = (f32[1,4,128]{2,1,0:T(4,128)S(1)}, f32[1,4,128]{2,1,0:T(4,128)}, u32[]{:S(2)}) copy-start(f32[1,4,128]{2,1,0:T(4,128)} %param.7) | copy-start | bytes 6148
  2.6 0.9 %copy-start = (bf16[1,128,1024]{2,1,0:T(8,128)(2,1)S(1)}, bf16[1,128,1024]{2,1,0:T(8,128)(2,1)}, u32[]{:S(2)}) copy-start(bf16[1,128,1024]{2,1,0:T(8,128)(2,1)} %param.6) | copy-start | bytes 786436
  3.6 0.7 %copy-start.3 = (s32[8,3]{0,1:T(4,128)S(1)}, s32[8,3]{0,1:T(4,128)}, u32[]{:S(2)}) copy-start(s32[8,3]{0,1:T(4,128)} %param.11) | copy-start | bytes 292

commit v4 on v3

--- a/solution.py
+++ b/solution.py
@@ -235,6 +235,7 @@
     mean_sum,
     grad_acc,
     grad_send,
+    in_sems,
     img_send,
     img_recv,
     halo_send,
@@ -262,6 +263,8 @@
             src_ref=src, dst_ref=dst, send_sem=send, recv_sem=recv, device_id=where, device_id_type=MESH
         )
 
+    own_in = pltpu.make_async_copy(images, img_ext.at[pl.ds(BLOCK, rows)], in_sems.at[0])
+    own_in.start()
     barrier = pltpu.get_barrier_semaphore()
     for step in range(1, n):
         pl.semaphore_signal(
@@ -354,7 +357,7 @@
         parts.append(part)
         rest = rest - part.astype(f32)
 
-    img_ext[BLOCK : rows + BLOCK] = images[...]
+    own_in.wait()
     exchange_wait(img_up, img_down)
     row_warped = jnp.zeros((rows, width), f32)
     for part in reversed(parts):
@@ -485,24 +488,33 @@
     lax.fori_loop(0, n, finish, 0)
     grad_ext[me + 1] = grad_send[me]
 
-    def drain(step, carry):
-        sec = lax.rem(me + step, n)
-
-        @pl.when(step > 0)
-        def _():
-            window_copy(sec).wait_send()
-            back_copy(sec).wait_send()
-            remote(
-                grad_send.at[sec], grad_ext.at[sec + 1], back_send.at[sec], back_recv.at[sec], {"sec": sec}
-            ).wait_recv()
-
-        return carry
-
-    lax.fori_loop(0, n, drain, 0)
+    def take_back(sec):
+        remote(
+            grad_send.at[sec], grad_ext.at[sec + 1], back_send.at[sec], back_recv.at[sec], {"sec": sec}
+        ).wait_recv()
+
+    for sec in (0, n - 1):
+
+        @pl.when(me != sec)
+        def _():
+            take_back(sec)
 
     edge_up = remote(grad_ext.at[1], grad_ext.at[n + 1], edge_send.at[0], edge_recv.at[1], up)
     edge_down = remote(grad_ext.at[n], grad_ext.at[0], edge_send.at[1], edge_recv.at[0], down)
     exchange_start(edge_up, edge_down)
+
+    def drain(step, carry):
+        sec = lax.rem(me + step, n)
+        window_copy(sec).wait_send()
+        back_copy(sec).wait_send()
+
+        @pl.when((sec > 0) & (sec < n - 1))
+        def _():
+            take_back(sec)
+
+        return carry
+
+    lax.fori_loop(1, n, drain, 0)
     exchange_wait(edge_up, edge_down)
     grad_done[...] = grad_ext[...]
     warp_done[...] = warp_ext[...]
@@ -568,7 +580,7 @@
             jax.ShapeDtypeStruct((n + 2, BLOCK, width), bf16),
             jax.ShapeDtypeStruct((2 * n + 2, BLOCK, width // 2), bf16),
         ),
-        in_specs=[vmem, vmem, smem, vmem, smem, smem],
+        in_specs=[where, vmem, smem, vmem, smem, smem],
         out_specs=(vmem, vmem),
         scratch_shapes=[
             pltpu.VMEM((n + 2, BLOCK, width), bf16),
@@ -583,6 +595,7 @@
             pltpu.VMEM((n, mid_rows, width), f32),
             pltpu.VMEM((n, BLOCK, width), f32),
             pltpu.VMEM((n, BLOCK, width), bf16),
+            dma((1,)),
             dma((2,)),
             dma((2,)),
             dma((2,)),
@@ -595,7 +608,7 @@
             dma((2,)),
         ],
         compiler_params=pltpu.CompilerParams(
-            collective_id=0, has_side_effects=True, vmem_limit_bytes=40 * 1024 * 1024
+            collective_id=0, has_side_effects=True, vmem_limit_bytes=61500 * 1024
         ),
     )(images[0], row_weights[0], row_shift, col_weights[0], col_shift, pair_on.T)
     return pl.pallas_call(
@@ -612,7 +625,7 @@
             pltpu.VMEM((2 * rows, width), bf16),
             dma((3,)),
         ],
-        compiler_params=pltpu.CompilerParams(vmem_limit_bytes=40 * 1024 * 1024),
+        compiler_params=pltpu.CompilerParams(vmem_limit_bytes=61500 * 1024),
     )(grad_ext, warp_ext)
 
 

time: 40 us -> 40 us (level)
  Pallas kernels: 35.5 us -> 37.9 us
  local copies, waits for them, and re-layouts: 2.3 us -> 0 us
    unnamed x8 -> x0, local copies, waits for them, and re-layouts: 2.3 us -> none
    pallas_call x1, Pallas kernels: 33.3 us -> 34.6 us  [fused(): pl.pallas_call(functools.partial(align_kernel, n, strips), out_shape=(jax...]
    pallas_call x1, Pallas kernels: 2.22 us -> 3.28 us  [fused(): pl.pallas_call(functools.partial(displace_kernel, n), out_shape=(jax.Shap...]
where the time goes in v4:
time: 40 us; the launch traced here: 39.8 us
  Pallas kernels  37.9 us (95%)
  between operations  1.93 us (5%)
    pallas_call x1, Pallas kernels, fused(): pl.pallas_call(functools.partial(align_kernel, n, strips), out_shape=(jax...  34.6 us
    pallas_call x1, Pallas kernels, fused(): pl.pallas_call(functools.partial(displace_kernel, n), out_shape=(jax.Shap...  3.28 us

profile of v4, /device:TPU:0, one launch (start us, length us, event | category | flops | bytes accessed | tf_op | source)
XLA Modules:
  0.0 39.8 jit_solution(12533934883548220578)
XLA Ops:
  1.9 34.6 %shard_map.77 = (bf16[10,16,1024]{2,1,0:T(8,128)(2,1)}, bf16[18,16,512]{2,1,0:T(8,128)(2,1)}) custom-call(bf16[128,1024]{1,0:T(8,128)(2,1)} %bitcast.4, f32[4,128]{1,0:T(4,128)} %bitcast.6, s32[1,1]{1,0:T(1,128)S(6)} %copy.8.row_shift, bf16[4,1024]{1,0:T(4,128)(2,1)} %bitcast.5, s32[1]{0:T(128)S(6)} %copy.9.col_shift, s32[3,8]{1,0:T(4,128)} %bitcast.7), custom_call_target="tpu_custom_call" | custom-call | tf_op jit(solution)/shard_map/pallas_call | solution.py:577
  36.5 3.3 %shard_map.78 = (f32[1,128,1024]{2,1,0:T(8,128)}, f32[2,1,128,1024]{3,2,1,0:T(8,128)}) custom-call(bf16[10,16,1024]{2,1,0:T(8,128)(2,1)} %get-tuple-element.4.grad_ext, bf16[18,16,512]{2,1,0:T(8,128)(2,1)} %get-tuple-element.5.warp_ext), custom_call_target="tpu_custom_call" | custom-call | tf_op jit(solution)/shard_map/pallas_call | solution.py:614
